TPU v7x, 32 devices: a whole 2x2x4 slice. The times are simulated.
32 devices in a mesh: ply: 4 (over y, x), tile: 8 (over z, core).
Axes of the slice: x: 2, y: 2, z: 4, core: 2. Of those that a mesh axis runs over, the one named last changes fastest.
Arguments:
- scaled_warmth: float32 [16, 64, 1024], P('ply', 'tile'), may hold values from 0.9 to 1.1
- crosslink_fraction: float32 [16, 64, 1024], P('ply', 'tile'), may hold values from 0 to 0.4
- fluid_stress: float32 [16, 64, 1024], P('ply', 'tile'), may hold values from 0 to 1
- preform_porosity_coefficient: float32 [16, 64, 1024], P('ply', 'tile'), may hold values from 0.02 to 0.2
- wetted_flags: int32 [16, 64, 1024], P('ply', 'tile'), may hold values 0 or 1
- injection_flags: int32 [16, 64, 1024], P('ply', 'tile'), may hold values 0 or 1
- outlet_flags: int32 [16, 64, 1024], P('ply', 'tile'), may hold values 0 or 1
Outputs:
- temperature_out: float32 [16, 64, 1024], P('ply', 'tile')
- cure_out: float32 [16, 64, 1024], P('ply', 'tile')
- pressure_out: float32 [16, 64, 1024], P('ply', 'tile')
- imbalance_record: float32 [2], replicated
All inputs are finite; a program needn't handle non-finite values. No bound on the sum of `wetted_flags` or of `injection_flags` or of `outlet_flags` on one device may be relied on, other than what follows from the above.
Results may differ from a plain program's by a relative error of at most 0.0003.
Values sent between devices are 32-bit elements; how exact they have to be, the bound alone decides.
A program may use at most 64 MiB of HBM per device.

v0:
```python
import jax
import jax.numpy as jnp
from jax import lax
from jax.sharding import PartitionSpec as P

STEPS = 2
SWEEPS = 4


fluidity_barrier = 4.0
fluidity_gelation_coefficient = 2.0
arrhenius_prefactor = 0.2
arrhenius_barrier = 8.0
released_enthalpy = 0.3
diffusion_coefficient = 0.1
clock_step_size = 0.5
epsilon = 1e-06


def with_halo(cells, sides, width):
    for axis, dim in sides:
        count = lax.axis_size(axis)
        ends = count - 1
        head = lax.slice_in_dim(cells, 0, width, axis=dim)
        tail = lax.slice_in_dim(cells, cells.shape[dim] - width, cells.shape[dim], axis=dim)
        cells = jnp.concatenate(
            [
                lax.ppermute(tail, axis, [(i, (i + 1) % count) for i in range(ends)]),
                cells,
                lax.ppermute(head, axis, [((i + 1) % count, i) for i in range(ends)]),
            ],
            axis=dim,
        )
    return cells


def interior(array):
    return array[1:-1, 1:-1, 1:-1]


def nearby_sites(array):
    return [
        array[2:, 1:-1, 1:-1],
        array[:-2, 1:-1, 1:-1],
        array[1:-1, 2:, 1:-1],
        array[1:-1, :-2, 1:-1],
        array[1:-1, 1:-1, 2:],
        array[1:-1, 1:-1, :-2],
    ]


def pad_across(array, width):
    return jnp.pad(array, [(0, 0)] * (array.ndim - 1) + [(width, width)])


def face_mobility(mobility_pad):
    centre = interior(mobility_pad)
    result = []
    for beside in nearby_sites(mobility_pad):
        denom = centre + beside
        result.append(2.0 * centre * beside / jnp.where(denom > 0, denom, 1.0))
    return result


def jacobi_sweep(pressure_pad, boundary_sides, dry_site, fixed_value):
    beside = nearby_sites(pressure_pad)
    weighted = boundary_sides[0] * beside[0]
    diagonal_sum = boundary_sides[0]
    for iteration_counter in range(1, 6):
        weighted = weighted + boundary_sides[iteration_counter] * beside[iteration_counter]
        diagonal_sum = diagonal_sum + boundary_sides[iteration_counter]
    return jnp.where(
        dry_site > 0, weighted / jnp.where(dry_site > 0, diagonal_sum, 1.0), fixed_value
    )


def donor_advection(
    fluid_stress,
    scaled_warmth,
    crosslink_fraction,
    boundary_sides,
    nearby_stress,
    nearby_warmth,
    nearby_crosslink,
    wetted_status,
    nearby_wetted,
    dry_site,
):
    weighted = boundary_sides[0] * nearby_stress[0]
    diagonal_sum = boundary_sides[0]
    for iteration_counter in range(1, 6):
        weighted = weighted + boundary_sides[iteration_counter] * nearby_stress[iteration_counter]
        diagonal_sum = diagonal_sum + boundary_sides[iteration_counter]
    darcy_imbalance = dry_site * (weighted - diagonal_sum * fluid_stress)
    donor_warmth_advance = jnp.zeros_like(scaled_warmth)
    donor_crosslink_advance = jnp.zeros_like(scaled_warmth)
    diffusive_stream = jnp.zeros_like(scaled_warmth)
    for iteration_counter in range(6):
        inward_stream = (
            jnp.maximum(
                boundary_sides[iteration_counter]
                * (nearby_stress[iteration_counter] - fluid_stress),
                0.0,
            )
            * nearby_wetted[iteration_counter]
        )
        donor_warmth_advance = donor_warmth_advance + inward_stream * (
            nearby_warmth[iteration_counter] - scaled_warmth
        )
        donor_crosslink_advance = donor_crosslink_advance + inward_stream * (
            nearby_crosslink[iteration_counter] - crosslink_fraction
        )
        diffusive_stream = diffusive_stream + nearby_wetted[iteration_counter] * (
            nearby_warmth[iteration_counter] - scaled_warmth
        )
    crosslink_speed = (
        arrhenius_prefactor
        * jnp.exp(arrhenius_barrier * (1.0 - 1.0 / scaled_warmth))
        * (1.0 - crosslink_fraction)
    )
    advanced_warmth = scaled_warmth + wetted_status * clock_step_size * (
        donor_warmth_advance
        + diffusion_coefficient * diffusive_stream
        + released_enthalpy * crosslink_speed
    )
    advanced_crosslink = crosslink_fraction + wetted_status * clock_step_size * (
        donor_crosslink_advance + crosslink_speed
    )
    return (darcy_imbalance, advanced_warmth, advanced_crosslink)


def per_device(
    scaled_warmth,
    crosslink_fraction,
    fluid_stress,
    preform_porosity_coefficient,
    wetted_flags,
    injection_flags,
    outlet_flags,
):
    wetted_status = wetted_flags.astype(jnp.float32)
    inlet_cell = injection_flags.astype(jnp.float32)
    dry_site = wetted_status * (1.0 - inlet_cell) * (1.0 - outlet_flags.astype(jnp.float32))
    site_total = scaled_warmth.size * lax.axis_size("ply") * lax.axis_size("tile")
    flag_pad = with_halo(
        jnp.stack((wetted_flags, injection_flags, outlet_flags)), (("ply", 1), ("tile", 2)), 2
    )
    flag_pad = pad_across(flag_pad, 2).astype(jnp.float32)
    free_cycle = interior(flag_pad[0] * (1.0 - flag_pad[1]) * (1.0 - flag_pad[2]))
    fixed_cycle = interior(flag_pad[1])
    fill_pad = interior(flag_pad[0])
    nearby_wetted = nearby_sites(fill_pad)
    gathered_magnitudes = []
    for repeat in range(STEPS):
        fluid_conductance = preform_porosity_coefficient * jnp.exp(
            -(
                fluidity_barrier * (1.0 / scaled_warmth - 1.0)
                + fluidity_gelation_coefficient * crosslink_fraction
            )
        )
        mobility_pad = pad_across(with_halo(fluid_conductance, (("ply", 0), ("tile", 1)), 2), 2)
        cycle_faces = face_mobility(mobility_pad)
        boundary_sides = [interior(face) for face in cycle_faces]
        for pair_index in range(SWEEPS // 2):
            pressure_pad = pad_across(with_halo(fluid_stress, (("ply", 0), ("tile", 1)), 2), 2)
            cycle_values = jacobi_sweep(pressure_pad, cycle_faces, free_cycle, fixed_cycle)
            fluid_stress = jacobi_sweep(cycle_values, boundary_sides, dry_site, inlet_cell)
        state_pad = with_halo(
            jnp.stack((fluid_stress, scaled_warmth, crosslink_fraction)),
            (("ply", 1), ("tile", 2)),
            1,
        )
        state_pad = pad_across(state_pad, 1)
        darcy_imbalance, scaled_warmth, crosslink_fraction = donor_advection(
            fluid_stress,
            scaled_warmth,
            crosslink_fraction,
            boundary_sides,
            nearby_sites(state_pad[0]),
            nearby_sites(state_pad[1]),
            nearby_sites(state_pad[2]),
            wetted_status,
            nearby_wetted,
            dry_site,
        )
        local_sum = jnp.sum(darcy_imbalance * darcy_imbalance)
        total = lax.psum(local_sum, ("ply", "tile"))
        gathered_magnitudes.append(jnp.sqrt(total / site_total + epsilon))
    imbalance_record = jnp.stack(gathered_magnitudes)
    return (scaled_warmth, crosslink_fraction, fluid_stress, imbalance_record)


def solution(mesh):
    return jax.shard_map(
        per_device,
        mesh=mesh,
        in_specs=(
            P("ply", "tile", None),
            P("ply", "tile", None),
            P("ply", "tile", None),
            P("ply", "tile", None),
            P("ply", "tile", None),
            P("ply", "tile", None),
            P("ply", "tile", None),
        ),
        out_specs=(P("ply", "tile", None), P("ply", "tile", None), P("ply", "tile", None), P()),
        check_vma=False,
    )
```

profile of v0, /device:TPU:0, one launch (start us, length us, event | category | flops | bytes accessed | tf_op | source)
XLA Modules:
  0.0 201.3 jit_solution(5231477649075351414)
XLA Ops:
  1.8 4.9 %collective-permute-start.4 = (s32[3,2,8,1024]{3,2,1,0:T(8,128)S(1)}, s32[3,2,8,1024]{3,2,1,0:T(8,128)S(1)}, u32[]{:S(2)}, u32[]{:S(2)}) collective-permute-start(s32[3,2,8,1024]{3,2,1,0:T(8,128)S(1)} %get-tuple-element.59), channel_id=1, source_target_pairs={{0,8},{8,16},{16,24},{1,9},{9,17},{17,25},{2,10},{10,18},{18,26},{... | collective-permute-start | bytes 589832 | tf_op jit(solution)/shard_map/ppermute | solution.py:28
  8.1 4.7 %collective-permute-start = (f32[2,8,1024]{2,1,0:T(8,128)S(1)}, f32[2,8,1024]{2,1,0:T(8,128)S(1)}, u32[]{:S(2)}, u32[]{:S(2)}) collective-permute-start(f32[2,8,1024]{2,1,0:T(8,128)S(1)} %get-tuple-element.81), channel_id=1, source_target_pairs={{0,8},{8,16},{16,24},{1,9},{9,17},{17,25},{2,10},{10,18},{18,26},{... | collective-permute-start | bytes 196616 | tf_op jit(solution)/shard_map/ppermute | solution.py:28
  14.1 4.9 %collective-permute-start.8 = (f32[2,8,1024]{2,1,0:T(8,128)S(1)}, f32[2,8,1024]{2,1,0:T(8,128)S(1)}, u32[]{:S(2)}, u32[]{:S(2)}) collective-permute-start(f32[2,8,1024]{2,1,0:T(8,128)S(1)} %get-tuple-element.84), channel_id=1, source_target_pairs={{0,8},{8,16},{16,24},{1,9},{9,17},{17,25},{2,10},{10,18},{18,26},{... | collective-permute-start | bytes 196616 | tf_op jit(solution)/shard_map/ppermute | solution.py:28
  23.1 3.1 %collective-permute-done.9 = f32[2,8,1024]{2,1,0:T(8,128)S(1)} collective-permute-done((f32[2,8,1024]{2,1,0:T(8,128)S(1)}, f32[2,8,1024]{2,1,0:T(8,128)S(1)}, u32[]{:S(2)}, u32[]{:S(2)}) %collective-permute-start.9) | collective-permute-done | bytes 65568 | tf_op jit(solution)/shard_map/ppermute | solution.py:30
  26.2 1.8 collective-permute-start.10
  30.0 4.3 %collective-permute-start.6 = (s32[3,8,2,1024]{3,2,1,0:T(2,128)S(1)}, s32[3,8,2,1024]{3,2,1,0:T(2,128)S(1)}, u32[]{:S(2)}, u32[]{:S(2)}) collective-permute-start(s32[3,8,2,1024]{3,2,1,0:T(2,128)S(1)} %get-tuple-element.49), channel_id=1, source_target_pairs={{0,1},{1,2},{2,3},{3,4},{4,5},{5,6},{6,7},{8,9},{9,10},{10,11},{11... | collective-permute-start | bytes 589832 | tf_op jit(solution)/shard_map/ppermute | solution.py:28
  36.0 2.8 %collective-permute-done.7 = s32[3,8,2,1024]{3,2,1,0:T(2,128)S(1)} collective-permute-done((s32[3,8,2,1024]{3,2,1,0:T(2,128)S(1)}, s32[3,8,2,1024]{3,2,1,0:T(2,128)S(1)}, u32[]{:S(2)}, u32[]{:S(2)}) %collective-permute-start.7) | collective-permute-done | bytes 196640 | tf_op jit(solution)/shard_map/ppermute | solution.py:30
  39.8 1.8 fusion.38
  42.1 5.4 %collective-permute-start.12 = (f32[2,8,1024]{2,1,0:T(8,128)S(1)}, f32[2,8,1024]{2,1,0:T(8,128)S(1)}, u32[]{:S(2)}, u32[]{:S(2)}) collective-permute-start(f32[2,8,1024]{2,1,0:T(8,128)S(1)} %get-tuple-element.79), channel_id=1, source_target_pairs={{0,8},{8,16},{16,24},{1,9},{9,17},{17,25},{2,10},{10,18},{18,26},{... | collective-permute-start | bytes 196616 | tf_op jit(solution)/shard_map/ppermute | solution.py:28
  49.4 5.2 %collective-permute-done.13 = f32[2,8,1024]{2,1,0:T(8,128)S(1)} collective-permute-done((f32[2,8,1024]{2,1,0:T(8,128)S(1)}, f32[2,8,1024]{2,1,0:T(8,128)S(1)}, u32[]{:S(2)}, u32[]{:S(2)}) %collective-permute-start.13) | collective-permute-done | bytes 65568 | tf_op jit(solution)/shard_map/ppermute | solution.py:30
  54.6 4.9 %collective-permute-start.14 = (f32[8,2,1024]{2,1,0:T(2,128)S(1)}, f32[8,2,1024]{2,1,0:T(2,128)S(1)}, u32[]{:S(2)}, u32[]{:S(2)}) collective-permute-start(f32[8,2,1024]{2,1,0:T(2,128)S(1)} %get-tuple-element.67), channel_id=1, source_target_pairs={{0,1},{1,2},{2,3},{3,4},{4,5},{5,6},{6,7},{8,9},{9,10},{10,11},{11... | collective-permute-start | bytes 196616 | tf_op jit(solution)/shard_map/ppermute | solution.py:28
  60.9 2.3 %collective-permute-done.15 = f32[8,2,1024]{2,1,0:T(2,128)S(1)} collective-permute-done((f32[8,2,1024]{2,1,0:T(2,128)S(1)}, f32[8,2,1024]{2,1,0:T(2,128)S(1)}, u32[]{:S(2)}, u32[]{:S(2)}) %collective-permute-start.15) | collective-permute-done | bytes 65568 | tf_op jit(solution)/shard_map/ppermute | solution.py:30
  65.1 5.0 %collective-permute-start.16 = (f32[3,1,8,1024]{3,2,1,0:T(8,128)S(1)}, f32[3,1,8,1024]{3,2,1,0:T(8,128)S(1)}, u32[]{:S(2)}, u32[]{:S(2)}) collective-permute-start(f32[3,1,8,1024]{3,2,1,0:T(8,128)S(1)} %get-tuple-element.57), channel_id=1, source_target_pairs={{0,8},{8,16},{16,24},{1,9},{9,17},{17,25},{2,10},{10,18},{18,26},{... | collective-permute-start | bytes 294920 | tf_op jit(solution)/shard_map/ppermute | solution.py:28
  72.2 4.3 %collective-permute-done.17 = f32[3,1,8,1024]{3,2,1,0:T(8,128)S(1)} collective-permute-done((f32[3,1,8,1024]{3,2,1,0:T(8,128)S(1)}, f32[3,1,8,1024]{3,2,1,0:T(8,128)S(1)}, u32[]{:S(2)}, u32[]{:S(2)}) %collective-permute-start.17) | collective-permute-done | bytes 98336 | tf_op jit(solution)/shard_map/ppermute | solution.py:30
  76.7 3.4 %collective-permute-start.18 = (f32[3,6,1,1024]{3,2,1,0:T(1,128)S(1)}, f32[3,6,1,1024]{3,2,1,0:T(1,128)S(1)}, u32[]{:S(2)}, u32[]{:S(2)}) collective-permute-start(f32[3,6,1,1024]{3,2,1,0:T(1,128)S(1)} %get-tuple-element.53), channel_id=1, source_target_pairs={{0,1},{1,2},{2,3},{3,4},{4,5},{5,6},{6,7},{8,9},{9,10},{10,11},{11... | collective-permute-start | bytes 221192 | tf_op jit(solution)/shard_map/ppermute | solution.py:28
  81.4 3.1 %collective-permute-start.24 = (f32[2,8,1024]{2,1,0:T(8,128)S(1)}, f32[2,8,1024]{2,1,0:T(8,128)S(1)}, u32[]{:S(2)}, u32[]{:S(2)}) collective-permute-start(f32[2,8,1024]{2,1,0:T(8,128)S(1)} %get-tuple-element.77), channel_id=1, source_target_pairs={{0,8},{8,16},{16,24},{1,9},{9,17},{17,25},{2,10},{10,18},{18,26},{... | collective-permute-start | bytes 196616 | tf_op jit(solution)/shard_map/ppermute | solution.py:28
  88.1 4.5 %collective-permute-start.20 = (f32[2,8,1024]{2,1,0:T(8,128)S(1)}, f32[2,8,1024]{2,1,0:T(8,128)S(1)}, u32[]{:S(2)}, u32[]{:S(2)}) collective-permute-start(f32[2,8,1024]{2,1,0:T(8,128)S(1)} %get-tuple-element.75), channel_id=1, source_target_pairs={{0,8},{8,16},{16,24},{1,9},{9,17},{17,25},{2,10},{10,18},{18,26},{... | collective-permute-start | bytes 196616 | tf_op jit(solution)/shard_map/ppermute | solution.py:28
  94.1 3.1 %collective-permute-start.26 = (f32[8,2,1024]{2,1,0:T(2,128)S(1)}, f32[8,2,1024]{2,1,0:T(2,128)S(1)}, u32[]{:S(2)}, u32[]{:S(2)}) collective-permute-start(f32[8,2,1024]{2,1,0:T(2,128)S(1)} %get-tuple-element.65), channel_id=1, source_target_pairs={{0,1},{1,2},{2,3},{3,4},{4,5},{5,6},{6,7},{8,9},{9,10},{10,11},{11... | collective-permute-start | bytes 196616 | tf_op jit(solution)/shard_map/ppermute | solution.py:28
  99.3 4.4 %collective-permute-start.22 = (f32[8,2,1024]{2,1,0:T(2,128)S(1)}, f32[8,2,1024]{2,1,0:T(2,128)S(1)}, u32[]{:S(2)}, u32[]{:S(2)}) collective-permute-start(f32[8,2,1024]{2,1,0:T(2,128)S(1)} %get-tuple-element.63), channel_id=1, source_target_pairs={{0,1},{1,2},{2,3},{3,4},{4,5},{5,6},{6,7},{8,9},{9,10},{10,11},{11... | collective-permute-start | bytes 196616 | tf_op jit(solution)/shard_map/ppermute | solution.py:28
  103.7 1.5 collective-permute-start.23
  105.6 2.5 %collective-permute-done.23 = f32[8,2,1024]{2,1,0:T(2,128)S(1)} collective-permute-done((f32[8,2,1024]{2,1,0:T(2,128)S(1)}, f32[8,2,1024]{2,1,0:T(2,128)S(1)}, u32[]{:S(2)}, u32[]{:S(2)}) %collective-permute-start.23) | collective-permute-done | bytes 65568 | tf_op jit(solution)/shard_map/ppermute | solution.py:30
  108.5 1.6 fusion.24
  110.6 4.5 %collective-permute-start.28 = (f32[2,8,1024]{2,1,0:T(8,128)S(1)}, f32[2,8,1024]{2,1,0:T(8,128)S(1)}, u32[]{:S(2)}, u32[]{:S(2)}) collective-permute-start(f32[2,8,1024]{2,1,0:T(8,128)S(1)} %get-tuple-element.73), channel_id=1, source_target_pairs={{0,8},{8,16},{16,24},{1,9},{9,17},{17,25},{2,10},{10,18},{18,26},{... | collective-permute-start | bytes 196616 | tf_op jit(solution)/shard_map/ppermute | solution.py:28
  117.0 4.8 %collective-permute-done.29 = f32[2,8,1024]{2,1,0:T(8,128)S(1)} collective-permute-done((f32[2,8,1024]{2,1,0:T(8,128)S(1)}, f32[2,8,1024]{2,1,0:T(8,128)S(1)}, u32[]{:S(2)}, u32[]{:S(2)}) %collective-permute-start.29) | collective-permute-done | bytes 65568 | tf_op jit(solution)/shard_map/ppermute | solution.py:30
  121.9 3.0 %collective-permute-start.30 = (f32[8,2,1024]{2,1,0:T(2,128)S(1)}, f32[8,2,1024]{2,1,0:T(2,128)S(1)}, u32[]{:S(2)}, u32[]{:S(2)}) collective-permute-start(f32[8,2,1024]{2,1,0:T(2,128)S(1)} %get-tuple-element.61), channel_id=1, source_target_pairs={{0,1},{1,2},{2,3},{3,4},{4,5},{5,6},{6,7},{8,9},{9,10},{10,11},{11... | collective-permute-start | bytes 196616 | tf_op jit(solution)/shard_map/ppermute | solution.py:28
  126.1 2.7 %collective-permute-done.31 = f32[8,2,1024]{2,1,0:T(2,128)S(1)} collective-permute-done((f32[8,2,1024]{2,1,0:T(2,128)S(1)}, f32[8,2,1024]{2,1,0:T(2,128)S(1)}, u32[]{:S(2)}, u32[]{:S(2)}) %collective-permute-start.31) | collective-permute-done | bytes 65568 | tf_op jit(solution)/shard_map/ppermute | solution.py:30
  130.6 4.7 %collective-permute-start.32 = (f32[3,1,8,1024]{3,2,1,0:T(8,128)S(1)}, f32[3,1,8,1024]{3,2,1,0:T(8,128)S(1)}, u32[]{:S(2)}, u32[]{:S(2)}) collective-permute-start(f32[3,1,8,1024]{3,2,1,0:T(8,128)S(1)} %get-tuple-element.55), channel_id=1, source_target_pairs={{0,8},{8,16},{16,24},{1,9},{9,17},{17,25},{2,10},{10,18},{18,26},{... | collective-permute-start | bytes 294920 | tf_op jit(solution)/shard_map/ppermute | solution.py:28
  137.5 4.3 %collective-permute-done.33 = f32[3,1,8,1024]{3,2,1,0:T(8,128)S(1)} collective-permute-done((f32[3,1,8,1024]{3,2,1,0:T(8,128)S(1)}, f32[3,1,8,1024]{3,2,1,0:T(8,128)S(1)}, u32[]{:S(2)}, u32[]{:S(2)}) %collective-permute-start.33) | collective-permute-done | bytes 98336 | tf_op jit(solution)/shard_map/ppermute | solution.py:30
  142.0 3.4 %collective-permute-start.34 = (f32[3,6,1,1024]{3,2,1,0:T(1,128)S(1)}, f32[3,6,1,1024]{3,2,1,0:T(1,128)S(1)}, u32[]{:S(2)}, u32[]{:S(2)}) collective-permute-start(f32[3,6,1,1024]{3,2,1,0:T(1,128)S(1)} %get-tuple-element.51), channel_id=1, source_target_pairs={{0,1},{1,2},{2,3},{3,4},{4,5},{5,6},{6,7},{8,9},{9,10},{10,11},{11... | collective-permute-start | bytes 221192 | tf_op jit(solution)/shard_map/ppermute | solution.py:28
  147.8 1.7 collective-permute-done.35
  152.3 42.7 %all-reduce.9 = (f32[]{:T(128)}, f32[]{:T(128)}) all-reduce(f32[]{:T(128)} %multiply_reduce_fusion, f32[]{:T(128)} %multiply_reduce_fusion.1), channel_id=1, replica_groups=mesh['ply'=4,'tile'=8] {'ply','tile'}, use_global_device_ids=true, to_apply=%region_3.4 | all-reduce | flops 2 | bytes 16 | tf_op jit(solution)/shard_map/psum | solution.py:187
  196.4 3.3 %fusion.48 = (f32[4,8,1024]{2,1,0:T(8,128)}, f32[4,8,1024]{2,1,0:T(8,128)S(1)}, f32[4,8,1024]{2,1,0:T(8,128)S(1)}, f32[4,8,1024]{2,1,0:T(8,128)S(1)}, f32[4,8,10...) fusion(f32[4,8,1024]{2,1,0:T(8,128)S(1)} %get-tuple-element.21, ...), kind=kLoop, calls=%fused_computation.144 | loop fusion | flops 1703936 | bytes 4587520 | tf_op jit(solution)/shard_map/add | solution.py:126
  (114 shorter events, 44.0 us)
Async XLA Ops:
  1.8 27.9 %collective-permute-start.4 = (s32[3,2,8,1024]{3,2,1,0:T(8,128)S(1)}, s32[3,2,8,1024]{3,2,1,0:T(8,128)S(1)}, u32[]{:S(2)}, u32[]{:S(2)}) collective-permute-start(s32[3,2,8,1024]{3,2,1,0:T(8,128)S(1)} %get-tuple-element.59), channel_id=1, source_target_pairs={{0,8},{8,16},{16,24},{1,9},{9,17},{17,25},{2,10},{10,18},{18,26},{... | collective-permute-start | bytes 589832 | tf_op jit(solution)/shard_map/ppermute | solution.py:28
  6.7 23.1 %collective-permute-start.5 = (s32[3,2,8,1024]{3,2,1,0:T(8,128)S(1)}, s32[3,2,8,1024]{3,2,1,0:T(8,128)S(1)}, u32[]{:S(2)}, u32[]{:S(2)}) collective-permute-start(s32[3,2,8,1024]{3,2,1,0:T(8,128)S(1)} %get-tuple-element.60), channel_id=1, source_target_pairs={{8,0},{16,8},{24,16},{9,1},{17,9},{25,17},{10,2},{18,10},{26,18},{... | collective-permute-start | bytes 589832 | tf_op jit(solution)/shard_map/ppermute | solution.py:30
  8.1 10.9 %collective-permute-start = (f32[2,8,1024]{2,1,0:T(8,128)S(1)}, f32[2,8,1024]{2,1,0:T(8,128)S(1)}, u32[]{:S(2)}, u32[]{:S(2)}) collective-permute-start(f32[2,8,1024]{2,1,0:T(8,128)S(1)} %get-tuple-element.81), channel_id=1, source_target_pairs={{0,8},{8,16},{16,24},{1,9},{9,17},{17,25},{2,10},{10,18},{18,26},{... | collective-permute-start | bytes 196616 | tf_op jit(solution)/shard_map/ppermute | solution.py:28
  12.8 7.6 %collective-permute-start.1 = (f32[2,8,1024]{2,1,0:T(8,128)S(1)}, f32[2,8,1024]{2,1,0:T(8,128)S(1)}, u32[]{:S(2)}, u32[]{:S(2)}) collective-permute-start(f32[2,8,1024]{2,1,0:T(8,128)S(1)} %get-tuple-element.82), channel_id=1, source_target_pairs={{8,0},{16,8},{24,16},{9,1},{17,9},{25,17},{10,2},{18,10},{26,18},{... | collective-permute-start | bytes 196616 | tf_op jit(solution)/shard_map/ppermute | solution.py:30
  14.1 7.6 %collective-permute-start.8 = (f32[2,8,1024]{2,1,0:T(8,128)S(1)}, f32[2,8,1024]{2,1,0:T(8,128)S(1)}, u32[]{:S(2)}, u32[]{:S(2)}) collective-permute-start(f32[2,8,1024]{2,1,0:T(8,128)S(1)} %get-tuple-element.84), channel_id=1, source_target_pairs={{0,8},{8,16},{16,24},{1,9},{9,17},{17,25},{2,10},{10,18},{18,26},{... | collective-permute-start | bytes 196616 | tf_op jit(solution)/shard_map/ppermute | solution.py:28
  19.1 7.1 %collective-permute-start.9 = (f32[2,8,1024]{2,1,0:T(8,128)S(1)}, f32[2,8,1024]{2,1,0:T(8,128)S(1)}, u32[]{:S(2)}, u32[]{:S(2)}) collective-permute-start(f32[2,8,1024]{2,1,0:T(8,128)S(1)} %get-tuple-element.83), channel_id=1, source_target_pairs={{8,0},{16,8},{24,16},{9,1},{17,9},{25,17},{10,2},{18,10},{26,18},{... | collective-permute-start | bytes 196616 | tf_op jit(solution)/shard_map/ppermute | solution.py:30
  20.4 7.6 %collective-permute-start.2 = (f32[8,2,1024]{2,1,0:T(2,128)S(1)}, f32[8,2,1024]{2,1,0:T(2,128)S(1)}, u32[]{:S(2)}, u32[]{:S(2)}) collective-permute-start(f32[8,2,1024]{2,1,0:T(2,128)S(1)} %get-tuple-element.69), channel_id=1, source_target_pairs={{0,1},{1,2},{2,3},{3,4},{4,5},{5,6},{6,7},{8,9},{9,10},{10,11},{11... | collective-permute-start | bytes 196616 | tf_op jit(solution)/shard_map/ppermute | solution.py:28
  21.8 7.6 %collective-permute-start.3 = (f32[8,2,1024]{2,1,0:T(2,128)S(1)}, f32[8,2,1024]{2,1,0:T(2,128)S(1)}, u32[]{:S(2)}, u32[]{:S(2)}) collective-permute-start(f32[8,2,1024]{2,1,0:T(2,128)S(1)} %get-tuple-element.70), channel_id=1, source_target_pairs={{1,0},{2,1},{3,2},{4,3},{5,4},{6,5},{7,6},{9,8},{10,9},{11,10},{12... | collective-permute-start | bytes 196616 | tf_op jit(solution)/shard_map/ppermute | solution.py:30
  26.2 9.4 %collective-permute-start.10 = (f32[8,2,1024]{2,1,0:T(2,128)S(1)}, f32[8,2,1024]{2,1,0:T(2,128)S(1)}, u32[]{:S(2)}, u32[]{:S(2)}) collective-permute-start(f32[8,2,1024]{2,1,0:T(2,128)S(1)} %get-tuple-element.71), channel_id=1, source_target_pairs={{0,1},{1,2},{2,3},{3,4},{4,5},{5,6},{6,7},{8,9},{9,10},{10,11},{11... | collective-permute-start | bytes 196616 | tf_op jit(solution)/shard_map/ppermute | solution.py:28
  28.0 7.6 %collective-permute-start.11 = (f32[8,2,1024]{2,1,0:T(2,128)S(1)}, f32[8,2,1024]{2,1,0:T(2,128)S(1)}, u32[]{:S(2)}, u32[]{:S(2)}) collective-permute-start(f32[8,2,1024]{2,1,0:T(2,128)S(1)} %get-tuple-element.72), channel_id=1, source_target_pairs={{1,0},{2,1},{3,2},{4,3},{5,4},{6,5},{7,6},{9,8},{10,9},{11,10},{12... | collective-permute-start | bytes 196616 | tf_op jit(solution)/shard_map/ppermute | solution.py:30
  30.0 6.1 %collective-permute-start.6 = (s32[3,8,2,1024]{3,2,1,0:T(2,128)S(1)}, s32[3,8,2,1024]{3,2,1,0:T(2,128)S(1)}, u32[]{:S(2)}, u32[]{:S(2)}) collective-permute-start(s32[3,8,2,1024]{3,2,1,0:T(2,128)S(1)} %get-tuple-element.49), channel_id=1, source_target_pairs={{0,1},{1,2},{2,3},{3,4},{4,5},{5,6},{6,7},{8,9},{9,10},{10,11},{11... | collective-permute-start | bytes 589832 | tf_op jit(solution)/shard_map/ppermute | solution.py:28
  34.3 4.6 %collective-permute-start.7 = (s32[3,8,2,1024]{3,2,1,0:T(2,128)S(1)}, s32[3,8,2,1024]{3,2,1,0:T(2,128)S(1)}, u32[]{:S(2)}, u32[]{:S(2)}) collective-permute-start(s32[3,8,2,1024]{3,2,1,0:T(2,128)S(1)} %get-tuple-element.50), channel_id=1, source_target_pairs={{1,0},{2,1},{3,2},{4,3},{5,4},{6,5},{7,6},{9,8},{10,9},{11,10},{12... | collective-permute-start | bytes 589832 | tf_op jit(solution)/shard_map/ppermute | solution.py:30
  42.1 7.3 %collective-permute-start.12 = (f32[2,8,1024]{2,1,0:T(8,128)S(1)}, f32[2,8,1024]{2,1,0:T(8,128)S(1)}, u32[]{:S(2)}, u32[]{:S(2)}) collective-permute-start(f32[2,8,1024]{2,1,0:T(8,128)S(1)} %get-tuple-element.79), channel_id=1, source_target_pairs={{0,8},{8,16},{16,24},{1,9},{9,17},{17,25},{2,10},{10,18},{18,26},{... | collective-permute-start | bytes 196616 | tf_op jit(solution)/shard_map/ppermute | solution.py:28
  47.5 7.1 %collective-permute-start.13 = (f32[2,8,1024]{2,1,0:T(8,128)S(1)}, f32[2,8,1024]{2,1,0:T(8,128)S(1)}, u32[]{:S(2)}, u32[]{:S(2)}) collective-permute-start(f32[2,8,1024]{2,1,0:T(8,128)S(1)} %get-tuple-element.80), channel_id=1, source_target_pairs={{8,0},{16,8},{24,16},{9,1},{17,9},{25,17},{10,2},{18,10},{26,18},{... | collective-permute-start | bytes 196616 | tf_op jit(solution)/shard_map/ppermute | solution.py:30
  54.6 6.2 %collective-permute-start.14 = (f32[8,2,1024]{2,1,0:T(2,128)S(1)}, f32[8,2,1024]{2,1,0:T(2,128)S(1)}, u32[]{:S(2)}, u32[]{:S(2)}) collective-permute-start(f32[8,2,1024]{2,1,0:T(2,128)S(1)} %get-tuple-element.67), channel_id=1, source_target_pairs={{0,1},{1,2},{2,3},{3,4},{4,5},{5,6},{6,7},{8,9},{9,10},{10,11},{11... | collective-permute-start | bytes 196616 | tf_op jit(solution)/shard_map/ppermute | solution.py:28
  65.1 7.2 %collective-permute-start.16 = (f32[3,1,8,1024]{3,2,1,0:T(8,128)S(1)}, f32[3,1,8,1024]{3,2,1,0:T(8,128)S(1)}, u32[]{:S(2)}, u32[]{:S(2)}) collective-permute-start(f32[3,1,8,1024]{3,2,1,0:T(8,128)S(1)} %get-tuple-element.57), channel_id=1, source_target_pairs={{0,8},{8,16},{16,24},{1,9},{9,17},{17,25},{2,10},{10,18},{18,26},{... | collective-permute-start | bytes 294920 | tf_op jit(solution)/shard_map/ppermute | solution.py:28
  70.1 6.5 %collective-permute-start.17 = (f32[3,1,8,1024]{3,2,1,0:T(8,128)S(1)}, f32[3,1,8,1024]{3,2,1,0:T(8,128)S(1)}, u32[]{:S(2)}, u32[]{:S(2)}) collective-permute-start(f32[3,1,8,1024]{3,2,1,0:T(8,128)S(1)} %get-tuple-element.58), channel_id=1, source_target_pairs={{8,0},{16,8},{24,16},{9,1},{17,9},{25,17},{10,2},{18,10},{26,18},{... | collective-permute-start | bytes 294920 | tf_op jit(solution)/shard_map/ppermute | solution.py:30
  76.7 9.1 %collective-permute-start.18 = (f32[3,6,1,1024]{3,2,1,0:T(1,128)S(1)}, f32[3,6,1,1024]{3,2,1,0:T(1,128)S(1)}, u32[]{:S(2)}, u32[]{:S(2)}) collective-permute-start(f32[3,6,1,1024]{3,2,1,0:T(1,128)S(1)} %get-tuple-element.53), channel_id=1, source_target_pairs={{0,1},{1,2},{2,3},{3,4},{4,5},{5,6},{6,7},{8,9},{9,10},{10,11},{11... | collective-permute-start | bytes 221192 | tf_op jit(solution)/shard_map/ppermute | solution.py:28
  80.1 5.7 %collective-permute-start.19 = (f32[3,6,1,1024]{3,2,1,0:T(1,128)S(1)}, f32[3,6,1,1024]{3,2,1,0:T(1,128)S(1)}, u32[]{:S(2)}, u32[]{:S(2)}) collective-permute-start(f32[3,6,1,1024]{3,2,1,0:T(1,128)S(1)} %get-tuple-element.54), channel_id=1, source_target_pairs={{1,0},{2,1},{3,2},{4,3},{5,4},{6,5},{7,6},{9,8},{10,9},{11,10},{12... | collective-permute-start | bytes 221192 | tf_op jit(solution)/shard_map/ppermute | solution.py:30
  81.4 12.6 %collective-permute-start.24 = (f32[2,8,1024]{2,1,0:T(8,128)S(1)}, f32[2,8,1024]{2,1,0:T(8,128)S(1)}, u32[]{:S(2)}, u32[]{:S(2)}) collective-permute-start(f32[2,8,1024]{2,1,0:T(8,128)S(1)} %get-tuple-element.77), channel_id=1, source_target_pairs={{0,8},{8,16},{16,24},{1,9},{9,17},{17,25},{2,10},{10,18},{18,26},{... | collective-permute-start | bytes 196616 | tf_op jit(solution)/shard_map/ppermute | solution.py:28
  84.5 9.5 %collective-permute-start.25 = (f32[2,8,1024]{2,1,0:T(8,128)S(1)}, f32[2,8,1024]{2,1,0:T(8,128)S(1)}, u32[]{:S(2)}, u32[]{:S(2)}) collective-permute-start(f32[2,8,1024]{2,1,0:T(8,128)S(1)} %get-tuple-element.78), channel_id=1, source_target_pairs={{8,0},{16,8},{24,16},{9,1},{17,9},{25,17},{10,2},{18,10},{26,18},{... | collective-permute-start | bytes 196616 | tf_op jit(solution)/shard_map/ppermute | solution.py:30
  88.1 10.4 %collective-permute-start.20 = (f32[2,8,1024]{2,1,0:T(8,128)S(1)}, f32[2,8,1024]{2,1,0:T(8,128)S(1)}, u32[]{:S(2)}, u32[]{:S(2)}) collective-permute-start(f32[2,8,1024]{2,1,0:T(8,128)S(1)} %get-tuple-element.75), channel_id=1, source_target_pairs={{0,8},{8,16},{16,24},{1,9},{9,17},{17,25},{2,10},{10,18},{18,26},{... | collective-permute-start | bytes 196616 | tf_op jit(solution)/shard_map/ppermute | solution.py:28
  92.7 6.6 %collective-permute-start.21 = (f32[2,8,1024]{2,1,0:T(8,128)S(1)}, f32[2,8,1024]{2,1,0:T(8,128)S(1)}, u32[]{:S(2)}, u32[]{:S(2)}) collective-permute-start(f32[2,8,1024]{2,1,0:T(8,128)S(1)} %get-tuple-element.76), channel_id=1, source_target_pairs={{8,0},{16,8},{24,16},{9,1},{17,9},{25,17},{10,2},{18,10},{26,18},{... | collective-permute-start | bytes 196616 | tf_op jit(solution)/shard_map/ppermute | solution.py:30
  94.1 11.1 %collective-permute-start.26 = (f32[8,2,1024]{2,1,0:T(2,128)S(1)}, f32[8,2,1024]{2,1,0:T(2,128)S(1)}, u32[]{:S(2)}, u32[]{:S(2)}) collective-permute-start(f32[8,2,1024]{2,1,0:T(2,128)S(1)} %get-tuple-element.65), channel_id=1, source_target_pairs={{0,1},{1,2},{2,3},{3,4},{4,5},{5,6},{6,7},{8,9},{9,10},{10,11},{11... | collective-permute-start | bytes 196616 | tf_op jit(solution)/shard_map/ppermute | solution.py:28
  97.2 8.0 %collective-permute-start.27 = (f32[8,2,1024]{2,1,0:T(2,128)S(1)}, f32[8,2,1024]{2,1,0:T(2,128)S(1)}, u32[]{:S(2)}, u32[]{:S(2)}) collective-permute-start(f32[8,2,1024]{2,1,0:T(2,128)S(1)} %get-tuple-element.66), channel_id=1, source_target_pairs={{1,0},{2,1},{3,2},{4,3},{5,4},{6,5},{7,6},{9,8},{10,9},{11,10},{12... | collective-permute-start | bytes 196616 | tf_op jit(solution)/shard_map/ppermute | solution.py:30
  99.3 6.3 %collective-permute-start.22 = (f32[8,2,1024]{2,1,0:T(2,128)S(1)}, f32[8,2,1024]{2,1,0:T(2,128)S(1)}, u32[]{:S(2)}, u32[]{:S(2)}) collective-permute-start(f32[8,2,1024]{2,1,0:T(2,128)S(1)} %get-tuple-element.63), channel_id=1, source_target_pairs={{0,1},{1,2},{2,3},{3,4},{4,5},{5,6},{6,7},{8,9},{9,10},{10,11},{11... | collective-permute-start | bytes 196616 | tf_op jit(solution)/shard_map/ppermute | solution.py:28
  103.7 4.4 %collective-permute-start.23 = (f32[8,2,1024]{2,1,0:T(2,128)S(1)}, f32[8,2,1024]{2,1,0:T(2,128)S(1)}, u32[]{:S(2)}, u32[]{:S(2)}) collective-permute-start(f32[8,2,1024]{2,1,0:T(2,128)S(1)} %get-tuple-element.64), channel_id=1, source_target_pairs={{1,0},{2,1},{3,2},{4,3},{5,4},{6,5},{7,6},{9,8},{10,9},{11,10},{12... | collective-permute-start | bytes 196616 | tf_op jit(solution)/shard_map/ppermute | solution.py:30
  110.6 6.4 %collective-permute-start.28 = (f32[2,8,1024]{2,1,0:T(8,128)S(1)}, f32[2,8,1024]{2,1,0:T(8,128)S(1)}, u32[]{:S(2)}, u32[]{:S(2)}) collective-permute-start(f32[2,8,1024]{2,1,0:T(8,128)S(1)} %get-tuple-element.73), channel_id=1, source_target_pairs={{0,8},{8,16},{16,24},{1,9},{9,17},{17,25},{2,10},{10,18},{18,26},{... | collective-permute-start | bytes 196616 | tf_op jit(solution)/shard_map/ppermute | solution.py:28
  115.1 6.7 %collective-permute-start.29 = (f32[2,8,1024]{2,1,0:T(8,128)S(1)}, f32[2,8,1024]{2,1,0:T(8,128)S(1)}, u32[]{:S(2)}, u32[]{:S(2)}) collective-permute-start(f32[2,8,1024]{2,1,0:T(8,128)S(1)} %get-tuple-element.74), channel_id=1, source_target_pairs={{8,0},{16,8},{24,16},{9,1},{17,9},{25,17},{10,2},{18,10},{26,18},{... | collective-permute-start | bytes 196616 | tf_op jit(solution)/shard_map/ppermute | solution.py:30
  130.6 6.9 %collective-permute-start.32 = (f32[3,1,8,1024]{3,2,1,0:T(8,128)S(1)}, f32[3,1,8,1024]{3,2,1,0:T(8,128)S(1)}, u32[]{:S(2)}, u32[]{:S(2)}) collective-permute-start(f32[3,1,8,1024]{3,2,1,0:T(8,128)S(1)} %get-tuple-element.55), channel_id=1, source_target_pairs={{0,8},{8,16},{16,24},{1,9},{9,17},{17,25},{2,10},{10,18},{18,26},{... | collective-permute-start | bytes 294920 | tf_op jit(solution)/shard_map/ppermute | solution.py:28
  135.4 6.5 %collective-permute-start.33 = (f32[3,1,8,1024]{3,2,1,0:T(8,128)S(1)}, f32[3,1,8,1024]{3,2,1,0:T(8,128)S(1)}, u32[]{:S(2)}, u32[]{:S(2)}) collective-permute-start(f32[3,1,8,1024]{3,2,1,0:T(8,128)S(1)} %get-tuple-element.56), channel_id=1, source_target_pairs={{8,0},{16,8},{24,16},{9,1},{17,9},{25,17},{10,2},{18,10},{26,18},{... | collective-permute-start | bytes 294920 | tf_op jit(solution)/shard_map/ppermute | solution.py:30
  142.0 5.8 %collective-permute-start.34 = (f32[3,6,1,1024]{3,2,1,0:T(1,128)S(1)}, f32[3,6,1,1024]{3,2,1,0:T(1,128)S(1)}, u32[]{:S(2)}, u32[]{:S(2)}) collective-permute-start(f32[3,6,1,1024]{3,2,1,0:T(1,128)S(1)} %get-tuple-element.51), channel_id=1, source_target_pairs={{0,1},{1,2},{2,3},{3,4},{4,5},{5,6},{6,7},{8,9},{9,10},{10,11},{11... | collective-permute-start | bytes 221192 | tf_op jit(solution)/shard_map/ppermute | solution.py:28
  (15 other events, 268.6 us)
where the time goes:
time: 203 us; the launch traced here: 201 us
  starting transfers between devices  94.8 us (47%)
  blocking collectives  42.7 us (21%)
  waiting for transfers between devices  37.4 us (18%)
  other arithmetic  22.3 us (11%)
  between operations  2.89 us (1%)
    ppermute x18, starting transfers between devices, with_halo(): lax.ppermute(tail, axis, [(i, (i + 1) % count) for i in range(ends)])  71.4 us
    psum x1, blocking collectives, per_device(): total = lax.psum(local_sum, ('ply', 'tile'))  42.7 us
    ppermute x18, waiting for transfers between devices, with_halo(): lax.ppermute(head, axis, [((i + 1) % count, i) for i in range(ends)])  34.4 us
    ppermute x18, starting transfers between devices, with_halo(): lax.ppermute(head, axis, [((i + 1) % count, i) for i in range(ends)])  23.4 us
    select_n x8, other arithmetic, jacobi_sweep(): jnp.where(dry_site > 0, weighted / jnp.where(dry_site > 0, diagonal_sum,...  7.11 us
    concatenate x9, other arithmetic, with_halo(): jnp.concatenate([lax.ppermute(tail, axis, [(i, (i + 1) % count) for i in...  4.34 us
  transfers between devices with their start and end apart: 36, of which 15 were waited for; matrix products, arithmetic and copies ran while one was open for 2% of the time, Pallas kernels for 0%

commit v1 on v0

v1 whole, which is shorter than its diff:
```python
import functools

import jax
import jax.numpy as jnp
from jax import lax
from jax.experimental import pallas as pl
from jax.experimental.pallas import tpu as pltpu
from jax.sharding import PartitionSpec as P

STEPS = 2
SWEEPS = 4

fluidity_barrier = 4.0
fluidity_gelation_coefficient = 2.0
arrhenius_prefactor = 0.2
arrhenius_barrier = 8.0
released_enthalpy = 0.3
diffusion_coefficient = 0.1
clock_step_size = 0.5
epsilon = 1e-06

MESH = pl.DeviceIdType.MESH
PER_STEP = SWEEPS + 3
MESSAGES = 2 + STEPS * PER_STEP


def mobility_of(warmth, cure, preform):
    return preform * jnp.exp(
        -(fluidity_barrier * (1.0 / warmth - 1.0) + fluidity_gelation_coefficient * cure)
    )


def face(m, k):
    denom = m + k
    return 2.0 * m * k / jnp.where(denom > 0, denom, 1.0)


def kernel(
    n_ply, n_tile,
    t_in, c_in, p_in, k_in, w_in, i_in, o_in,
    t_out, c_out, p_out, rec_out,
    tb, cb, pb, mb, kb, flags, fill, free, fixed, fills, fz, fy, fx, fh, diag, inv, acc, part,
    hp, hr, red, half, tot,
    in_sem, out_sem, send_sem, recv_sem, rs_sem, rr_sem, qs_sem, qr_sem,
):
    planes, rows, width = p_in.shape
    ply, tile = lax.axis_index("ply"), lax.axis_index("tile")
    sites = planes * rows * width * n_ply * n_tile

    ins = [
        pltpu.make_async_copy(src, dst, in_sem.at[n])
        for n, (src, dst) in enumerate(
            [(p_in, pb.at[0]), (t_in, tb.at[0]), (c_in, cb.at[0]), (k_in, kb),
             (w_in, flags.at[0]), (i_in, flags.at[1]), (o_in, flags.at[2])]
        )
    ]
    for copy in ins:
        copy.start()

    barrier = pltpu.get_barrier_semaphore()
    for off in range(1, n_ply):
        pl.semaphore_signal(
            barrier, inc=1, device_id=(lax.rem(ply + off, n_ply), tile), device_id_type=MESH
        )

    def greet(off, carry):
        pl.semaphore_signal(
            barrier, inc=1, device_id=(ply, lax.rem(tile + off, n_tile)), device_id_type=MESH
        )
        return carry

    lax.fori_loop(1, n_tile, greet, 0)
    pl.semaphore_wait(barrier, n_ply + n_tile - 2)

    has = [ply < n_ply - 1, ply > 0, tile < n_tile - 1, tile > 0]

    def message(m, src, d):
        if d < 2:
            edge = 0 if d == 0 else planes - 1
            a, b = src.at[edge], hp.at[m, 1 - d]
            where = (ply - 1 if d == 0 else ply + 1, tile)
        else:
            lo, hi = pl.ds(0, 1), pl.ds(rows - 1, 1)
            a = src.at[:, lo if d == 2 else hi]
            b = hr.at[m, :, hi if d == 2 else lo]
            where = (ply, tile - 1 if d == 2 else tile + 1)
        return pltpu.make_async_remote_copy(
            src_ref=a, dst_ref=b, send_sem=send_sem.at[m, d], recv_sem=recv_sem.at[m, d],
            device_id=where, device_id_type=MESH,
        )

    opposite = [1, 0, 3, 2]

    def send(m, src, ds=(0, 1, 2, 3)):
        for d in ds:
            pl.when(has[opposite[d]])(lambda d=d: message(m, src, d).start())

    def landed(m, src, ds):
        for d in ds:
            pl.when(has[d])(lambda d=d: message(m, src, d).wait_recv())

    def sent(m, src):
        for d in range(4):
            pl.when(has[opposite[d]])(lambda d=d: message(m, src, d).wait_send())

    row = lax.broadcasted_iota(jnp.int32, (rows, width), 0)
    lane = lax.broadcasted_iota(jnp.int32, (rows, width), 1)
    first_row, last_row = row == 0, row == rows - 1
    edge_row = (first_row & (tile > 0)) | (last_row & (tile < n_tile - 1))
    first_lane, last_lane = lane == 0, lane == width - 1

    def up(x, axis):
        return pltpu.roll(x, x.shape[axis] - 1, axis)

    def down(x, axis):
        return pltpu.roll(x, 1, axis)

    def low_plane(m):
        return jnp.where(ply > 0, hp[m, 0], 0.0)

    def high_plane(m):
        return jnp.where(ply < n_ply - 1, hp[m, 1], 0.0)

    def edge_rows(m, p):
        return jnp.where(edge_row, hr[m, p], 0.0)

    P0, FILL = 0, 1
    MOB = [2 + s * PER_STEP for s in range(STEPS)]
    WARM = [m + 1 for m in MOB]
    CURE = [m + 2 for m in MOB]
    PRESS = [[MOB[s] + 3 + k for k in range(SWEEPS)] for s in range(STEPS)]
    sources = {P0: pb.at[0], FILL: fill}
    for s in range(STEPS):
        sources[MOB[s]], sources[WARM[s]], sources[CURE[s]] = mb.at[s], tb.at[s], cb.at[s]
        for k in range(SWEEPS):
            sources[PRESS[s][k]] = pb.at[s * SWEEPS + k + 1]

    def reduce_send(s):
        def body(off, carry):
            pltpu.make_async_remote_copy(
                src_ref=part.at[s], dst_ref=red.at[s, tile],
                send_sem=rs_sem.at[s, off], recv_sem=rr_sem.at[s, tile],
                device_id=(ply, lax.rem(tile + off, n_tile)), device_id_type=MESH,
            ).start()
            return carry

        lax.fori_loop(1, n_tile, body, 0)

    def reduce_mid(s):
        def body(off, total):
            peer = lax.rem(tile + off, n_tile)
            copy = pltpu.make_async_remote_copy(
                src_ref=part.at[s], dst_ref=red.at[s, peer],
                send_sem=rs_sem.at[s, off], recv_sem=rr_sem.at[s, peer],
                device_id=(ply, peer), device_id_type=MESH,
            )
            copy.wait_recv()
            copy.wait_send()
            return total + red[s, peer]

        half[s] = lax.fori_loop(1, n_tile, body, part[s])
        for off in range(1, n_ply):
            pltpu.make_async_remote_copy(
                src_ref=half.at[s], dst_ref=tot.at[s, ply],
                send_sem=qs_sem.at[s, off], recv_sem=qr_sem.at[s, ply],
                device_id=(lax.rem(ply + off, n_ply), tile), device_id_type=MESH,
            ).start()

    def reduce_end(s):
        tot[s, ply] = half[s]
        for off in range(1, n_ply):
            peer = lax.rem(ply + off, n_ply)
            copy = pltpu.make_async_remote_copy(
                src_ref=half.at[s], dst_ref=tot.at[s, peer],
                send_sem=qs_sem.at[s, off], recv_sem=qr_sem.at[s, peer],
                device_id=(peer, tile), device_id_type=MESH,
            )
            copy.wait_recv()
            copy.wait_send()
        total = tot[s, 0]
        for j in range(1, n_ply):
            total = total + tot[s, j]
        root = jnp.sqrt(jnp.full((8, 128), jnp.sum(total)) / sites + epsilon)
        rec_out[s] = root[0, 0]

    ins[0].wait()
    send(P0, pb.at[0])
    for copy in ins[1:4]:
        copy.wait()
    for p in range(planes):
        mb[0, p] = mobility_of(tb[0, p], cb[0, p], kb[p])
    send(MOB[0], mb.at[0])
    for copy in ins[4:]:
        copy.wait()
    for p in range(planes):
        wet = flags[0, p].astype(jnp.float32)
        inlet = flags[1, p].astype(jnp.float32)
        loose = wet * (1.0 - inlet) * (1.0 - flags[2, p].astype(jnp.float32))
        fill[p] = wet
        free[p] = loose
        fixed[p] = jnp.where(loose > 0, 0.0, inlet)
        fills[0, p] = jnp.where(last_row, 0.0, up(wet, 0))
        fills[1, p] = jnp.where(first_row, 0.0, down(wet, 0))
        fills[2, p] = jnp.where(last_lane, 0.0, up(wet, 1))
        fills[3, p] = jnp.where(first_lane, 0.0, down(wet, 1))

    before = P0
    for s in range(STEPS):
        for p in range(planes):
            m = mb[s, p]
            if p:
                fz[p] = face(mb[s, p - 1], m)
            a = jnp.where(last_row, 0.0, face(m, up(m, 0)))
            fy[0, p] = a
            fy[1, p] = jnp.where(first_row, 0.0, down(a, 0))
            b = jnp.where(last_lane, 0.0, face(m, up(m, 1)))
            fx[0, p] = b
            fx[1, p] = jnp.where(first_lane, 0.0, down(b, 1))

        def inside(x):
            for p in range(planes):
                v = x[p]
                total = fx[0, p] * up(v, 1) + fx[1, p] * down(v, 1)
                total += fy[0, p] * up(v, 0) + fy[1, p] * down(v, 0)
                if p:
                    total += fz[p] * x[p - 1]
                if p < planes - 1:
                    total += fz[p + 1] * x[p + 1]
                acc[p] = total

        inside(pb.at[s * SWEEPS])
        landed(MOB[s], mb.at[s], (2, 3, 0, 1))
        fz[0] = face(mb[s, 0], low_plane(MOB[s]))
        fz[planes] = face(mb[s, planes - 1], high_plane(MOB[s]))
        for p in range(planes):
            beside = face(mb[s, p], edge_rows(MOB[s], p))
            fh[p] = beside
            total = fz[p] + fz[p + 1] + fy[0, p] + fy[1, p] + beside + fx[0, p] + fx[1, p]
            diag[p] = total
            moving = free[p] > 0
            inv[p] = jnp.where(moving, 1.0 / jnp.where(moving, total, 1.0), 0.0)

        order = list(range(1, planes - 1))
        for k in range(SWEEPS):
            old, new = pb.at[s * SWEEPS + k], pb.at[s * SWEEPS + k + 1]
            if s == 0 or k:
                landed(before, old, (2, 3))

            def finish(p):
                total = acc[p] + fh[p] * edge_rows(before, p)
                if p == 0:
                    total += fz[0] * low_plane(before)
                if p == planes - 1:
                    total += fz[planes] * high_plane(before)
                new[p] = total * inv[p] + fixed[p]

            for p in order:
                finish(p)
            if planes > 1:
                if s == 0 or k:
                    landed(before, old, (1,))
                finish(0)
                send(PRESS[s][k], new, (0,))
                if s == 0 or k:
                    landed(before, old, (0,))
                finish(planes - 1)
                send(PRESS[s][k], new, (1, 2, 3))
            else:
                if s == 0 or k:
                    landed(before, old, (0, 1))
                finish(0)
                send(PRESS[s][k], new)
            if k == 0:
                send(WARM[s], tb.at[s])
            if k == 1:
                send(CURE[s], cb.at[s])
            if k == 2 and s == 0:
                send(FILL, fill)
            if k == 1 and s:
                reduce_mid(s - 1)
            inside(new)
            before = PRESS[s][k]

        now = s * SWEEPS + SWEEPS
        if s == STEPS - 1:
            pltpu.make_async_copy(pb.at[now], p_out, out_sem.at[0]).start()
        landed(WARM[s], tb.at[s], (0, 1, 2, 3))
        landed(CURE[s], cb.at[s], (0, 1, 2, 3))
        if s == 0:
            landed(FILL, fill, (0, 1, 2, 3))

        def stream(p, f, press, warm, cure, wet):
            q = jnp.maximum(f * (press - pb[now, p]), 0.0) * wet
            dt = warm - tb[s, p]
            return (q + diffusion_coefficient * wet) * dt, q * (cure - cb[s, p])

        gained = []
        for p in range(planes):
            v, t, c = pb[now, p], tb[s, p], cb[s, p]
            speed = arrhenius_prefactor * jnp.exp(arrhenius_barrier * (1.0 - 1.0 / t)) * (1.0 - c)
            dt, dc = released_enthalpy * speed, speed
            for n, (move, axis, f) in enumerate(
                [(up, 0, fy[0, p]), (down, 0, fy[1, p]), (up, 1, fx[0, p]), (down, 1, fx[1, p])]
            ):
                a, b = stream(p, f, move(v, axis), move(t, axis), move(c, axis), fills[n, p])
                dt, dc = dt + a, dc + b
            for q, f in [(p - 1, fz[p]), (p + 1, fz[p + 1])]:
                if 0 <= q < planes:
                    a, b = stream(p, f, pb[now, q], tb[s, q], cb[s, q], fill[q])
                    dt, dc = dt + a, dc + b
            tb[s + 1, p] = dt
            cb[s + 1, p] = dc

        landed(before, pb.at[now], (2, 3, 0, 1))
        squares = jnp.zeros((rows, width), jnp.float32)
        for p in range(planes):
            total = acc[p] + fh[p] * edge_rows(before, p)
            if p == 0:
                total += fz[0] * low_plane(before)
            if p == planes - 1:
                total += fz[planes] * high_plane(before)
            off = free[p] * (total - diag[p] * pb[now, p])
            squares += off * off
        small = jnp.zeros((8, 128), jnp.float32)
        for r in range(0, rows, 8):
            for l in range(0, width, 128):
                small += squares[r:r + 8, l:l + 128]
        part[s] = small
        if s == STEPS - 1:
            reduce_send(s)
        for p in range(planes):
            dt, dc = tb[s + 1, p], cb[s + 1, p]
            ways = [(fh[p], edge_rows(before, p), edge_rows(WARM[s], p), edge_rows(CURE[s], p),
                     edge_rows(FILL, p))]
            if p == 0:
                ways.append((fz[0], low_plane(before), low_plane(WARM[s]), low_plane(CURE[s]),
                             low_plane(FILL)))
            if p == planes - 1:
                ways.append((fz[planes], high_plane(before), high_plane(WARM[s]),
                             high_plane(CURE[s]), high_plane(FILL)))
            for way in ways:
                a, b = stream(p, *way)
                dt, dc = dt + a, dc + b
            share = fill[p] * clock_step_size
            t = tb[s, p] + share * dt
            c = cb[s, p] + share * dc
            tb[s + 1, p] = t
            cb[s + 1, p] = c
            if s < STEPS - 1:
                mb[s + 1, p] = mobility_of(t, c, kb[p])
        if s < STEPS - 1:
            send(MOB[s + 1], mb.at[s + 1])
            reduce_send(s)

    outs = [
        pltpu.make_async_copy(pb.at[STEPS * SWEEPS], p_out, out_sem.at[0]),
        pltpu.make_async_copy(tb.at[STEPS], t_out, out_sem.at[1]),
        pltpu.make_async_copy(cb.at[STEPS], c_out, out_sem.at[2]),
    ]
    outs[1].start()
    outs[2].start()
    reduce_mid(STEPS - 1)
    for s in range(STEPS - 1):
        reduce_end(s)
    for m, src in sources.items():
        sent(m, src)
    reduce_end(STEPS - 1)
    for copy in outs:
        copy.wait()


def per_device(n_ply, n_tile, *fields):
    shape = fields[0].shape
    planes, rows, width = shape
    real = jnp.float32

    def block(*lead):
        return pltpu.VMEM((*lead, *shape), real)

    dma = pltpu.SemaphoreType.DMA
    scratch = [
        block(STEPS + 1), block(STEPS + 1), block(STEPS * SWEEPS + 1), block(STEPS), block(),
        pltpu.VMEM((3, *shape), jnp.int32), block(), block(), block(), block(4),
        pltpu.VMEM((planes + 1, rows, width), real), block(2), block(2), block(), block(), block(),
        block(), pltpu.VMEM((STEPS, 8, 128), real),
        pltpu.VMEM((MESSAGES, 2, rows, width), real), block(MESSAGES),
        pltpu.VMEM((STEPS, n_tile, 8, 128), real), pltpu.VMEM((STEPS, 8, 128), real),
        pltpu.VMEM((STEPS, n_ply, 8, 128), real),
        dma((7,)), dma((3,)), dma((MESSAGES, 4)), dma((MESSAGES, 4)),
        dma((STEPS, n_tile)), dma((STEPS, n_tile)), dma((STEPS, n_ply)), dma((STEPS, n_ply)),
    ]
    out = jax.ShapeDtypeStruct(shape, real)
    anywhere = pl.BlockSpec(memory_space=pl.ANY)
    return pl.pallas_call(
        functools.partial(kernel, n_ply, n_tile),
        out_shape=(out, out, out, jax.ShapeDtypeStruct((STEPS,), real)),
        in_specs=[anywhere] * 7,
        out_specs=(anywhere, anywhere, anywhere, pl.BlockSpec(memory_space=pltpu.SMEM)),
        scratch_shapes=scratch,
        compiler_params=pltpu.CompilerParams(
            collective_id=0, has_side_effects=True, vmem_limit_bytes=24 * 1024 * 1024
        ),
    )(*fields)


def solution(mesh):
    spec = P("ply", "tile", None)
    return jax.shard_map(
        functools.partial(per_device, mesh.shape["ply"], mesh.shape["tile"]),
        mesh=mesh,
        in_specs=(spec,) * 7,
        out_specs=(spec, spec, spec, P()),
        check_vma=False,
    )
```

time: 203 us -> 61.1 us (0.30)
  starting transfers between devices: 94.8 us -> 0 us
  Pallas kernels: 0 us -> 51.4 us
  blocking collectives: 42.7 us -> 0 us
  waiting for transfers between devices: 37.4 us -> 0 us
  other arithmetic: 22.3 us -> 0 us
  local copies, waits for them, and re-layouts: 1.35 us -> 8.8 us
  between operations: 2.89 us -> 0.66 us
    ppermute x36 -> x0, starting transfers between devices: 94.8 us -> none  [the longest x18 71.4 us: with_halo(): lax.ppermute(tail, axis, [(i, (i + 1) % count) for i in range(ends)])]
    pallas_call x0 -> x1, Pallas kernels: none -> 51.4 us  [per_device(): pl.pallas_call(functools.partial(kernel, n_ply, n_tile), out_shape=(out,...]
    psum x1 -> x0, blocking collectives: 42.7 us -> none  [per_device(): total = lax.psum(local_sum, ('ply', 'tile'))]
    ppermute x36 -> x0, waiting for transfers between devices: 37.4 us -> none  [the longest x18 34.4 us: with_halo(): lax.ppermute(head, axis, [((i + 1) % count, i) for i in range(ends)])]
    unnamed x24 -> x18, local copies, waits for them, and re-layouts: 0.07 us -> 8.8 us
    select_n x8 -> x0, other arithmetic: 7.11 us -> none  [jacobi_sweep(): jnp.where(dry_site > 0, weighted / jnp.where(dry_site > 0, diagonal_sum,...]
    add x2 -> x0, other arithmetic: 4.38 us -> none  [the longest x1 3.28 us: donor_advection(): crosslink_fraction + wetted_status * clock_step_size * (donor_crosslink_a...]
    concatenate x9 -> x0, other arithmetic: 4.34 us -> none  [with_halo(): jnp.concatenate([lax.ppermute(tail, axis, [(i, (i + 1) % count) for i in...]
  transfers between devices with their start and end apart: 36 -> 0, of which waited for: 15 -> 0; matrix products, arithmetic and copies ran while one was open for 2% -> 0% of each run, Pallas kernels for 0% -> 0%
where the time goes in v1:
time: 61.1 us; the launch traced here: 60.8 us
  Pallas kernels  51.4 us (84%)
  local copies, waits for them, and re-layouts  8.8 us (14%)
  between operations  0.66 us (1%)
    pallas_call x1, Pallas kernels, per_device(): pl.pallas_call(functools.partial(kernel, n_ply, n_tile), out_shape=(out,...  51.4 us
    unnamed x18, local copies, waits for them, and re-layouts  8.8 us

profile of v1, /device:TPU:0, one launch (start us, length us, event | category | flops | bytes accessed | tf_op | source)
XLA Modules:
  0.0 60.8 jit_solution(12078693217943128444)
XLA Ops:
  0.6 0.0 copy-start
  0.6 0.9 %copy-done = f32[4,8,1024]{2,1,0:T(8,128)S(1)} copy-done((f32[4,8,1024]{2,1,0:T(8,128)S(1)}, f32[4,8,1024]{2,1,0:T(8,128)}, u32[]{:S(2)}) %copy-start) | copy-done | bytes 131096
  1.5 0.0 copy-start.1
  1.5 0.9 %copy-done.1 = f32[4,8,1024]{2,1,0:T(8,128)S(1)} copy-done((f32[4,8,1024]{2,1,0:T(8,128)S(1)}, f32[4,8,1024]{2,1,0:T(8,128)}, u32[]{:S(2)}) %copy-start.1) | copy-done | bytes 131096
  2.4 0.0 copy-start.2
  2.4 0.9 %copy-done.2 = f32[4,8,1024]{2,1,0:T(8,128)S(1)} copy-done((f32[4,8,1024]{2,1,0:T(8,128)S(1)}, f32[4,8,1024]{2,1,0:T(8,128)}, u32[]{:S(2)}) %copy-start.2) | copy-done | bytes 131096
  3.3 0.0 copy-start.3
  3.4 0.9 %copy-done.3 = f32[4,8,1024]{2,1,0:T(8,128)S(1)} copy-done((f32[4,8,1024]{2,1,0:T(8,128)S(1)}, f32[4,8,1024]{2,1,0:T(8,128)}, u32[]{:S(2)}) %copy-start.3) | copy-done | bytes 131096
  4.3 0.0 copy-start.4
  4.3 0.9 %copy-done.4 = s32[4,8,1024]{2,1,0:T(8,128)S(1)} copy-done((s32[4,8,1024]{2,1,0:T(8,128)S(1)}, s32[4,8,1024]{2,1,0:T(8,128)}, u32[]{:S(2)}) %copy-start.4) | copy-done | bytes 131096
  5.2 0.0 copy-start.5
  5.2 0.9 %copy-done.5 = s32[4,8,1024]{2,1,0:T(8,128)S(1)} copy-done((s32[4,8,1024]{2,1,0:T(8,128)S(1)}, s32[4,8,1024]{2,1,0:T(8,128)}, u32[]{:S(2)}) %copy-start.5) | copy-done | bytes 131096
  6.1 0.0 copy-start.6
  6.1 0.9 %copy-done.6 = s32[4,8,1024]{2,1,0:T(8,128)S(1)} copy-done((s32[4,8,1024]{2,1,0:T(8,128)S(1)}, s32[4,8,1024]{2,1,0:T(8,128)}, u32[]{:S(2)}) %copy-start.6) | copy-done | bytes 131096
  7.0 51.4 %shard_map.102 = (f32[4,8,1024]{2,1,0:T(8,128)S(1)}, f32[4,8,1024]{2,1,0:T(8,128)S(1)}, f32[4,8,1024]{2,1,0:T(8,128)S(1)}, f32[2]{0:T(128)S(1)}) custom-call(f32[4,8,1024]{2,1,0:T(8,128)S(1)} %copy-done, f32[4,8,1024]{2,1,0:T(8,128)S(1)} %copy-done.1, f32[4,8,1024]{2,1,0:T(8,128)S(1)} %copy-done.2, f32[4,8,1024]{2,1,0:T(8,128)S(1)} %copy-done.3, ...), custom_call_target="tpu_custom_call" | custom-call | tf_op jit(solution)/shard_map/pallas_call | solution.py:394
  58.3 0.7 %copy.15 = f32[4,8,1024]{2,1,0:T(8,128)} copy(f32[4,8,1024]{2,1,0:T(8,128)S(1)} %get-tuple-element.8) | data formatting | bytes 262144
  59.0 0.7 %copy.16 = f32[4,8,1024]{2,1,0:T(8,128)} copy(f32[4,8,1024]{2,1,0:T(8,128)S(1)} %get-tuple-element.9) | data formatting | bytes 262144
  59.7 0.7 %copy.17 = f32[4,8,1024]{2,1,0:T(8,128)} copy(f32[4,8,1024]{2,1,0:T(8,128)S(1)} %get-tuple-element.10) | data formatting | bytes 262144
  60.3 0.5 copy.18
Async XLA Ops:
  0.6 0.9 %copy-start = (f32[4,8,1024]{2,1,0:T(8,128)S(1)}, f32[4,8,1024]{2,1,0:T(8,128)}, u32[]{:S(2)}) copy-start(f32[4,8,1024]{2,1,0:T(8,128)} %t_in.1) | copy-start | bytes 393220
  1.5 0.9 %copy-start.1 = (f32[4,8,1024]{2,1,0:T(8,128)S(1)}, f32[4,8,1024]{2,1,0:T(8,128)}, u32[]{:S(2)}) copy-start(f32[4,8,1024]{2,1,0:T(8,128)} %c_in.1) | copy-start | bytes 393220
  2.4 0.9 %copy-start.2 = (f32[4,8,1024]{2,1,0:T(8,128)S(1)}, f32[4,8,1024]{2,1,0:T(8,128)}, u32[]{:S(2)}) copy-start(f32[4,8,1024]{2,1,0:T(8,128)} %p_in.1) | copy-start | bytes 393220
  3.3 0.9 %copy-start.3 = (f32[4,8,1024]{2,1,0:T(8,128)S(1)}, f32[4,8,1024]{2,1,0:T(8,128)}, u32[]{:S(2)}) copy-start(f32[4,8,1024]{2,1,0:T(8,128)} %k_in.1) | copy-start | bytes 393220
  4.3 0.9 %copy-start.4 = (s32[4,8,1024]{2,1,0:T(8,128)S(1)}, s32[4,8,1024]{2,1,0:T(8,128)}, u32[]{:S(2)}) copy-start(s32[4,8,1024]{2,1,0:T(8,128)} %w_in.1) | copy-start | bytes 393220
  5.2 0.9 %copy-start.5 = (s32[4,8,1024]{2,1,0:T(8,128)S(1)}, s32[4,8,1024]{2,1,0:T(8,128)}, u32[]{:S(2)}) copy-start(s32[4,8,1024]{2,1,0:T(8,128)} %i_in.1) | copy-start | bytes 393220
  6.1 0.9 %copy-start.6 = (s32[4,8,1024]{2,1,0:T(8,128)S(1)}, s32[4,8,1024]{2,1,0:T(8,128)}, u32[]{:S(2)}) copy-start(s32[4,8,1024]{2,1,0:T(8,128)} %o_in.1) | copy-start | bytes 393220

commit v2 on v1

--- a/solution.py
+++ b/solution.py
@@ -20,8 +20,10 @@
 epsilon = 1e-06
 
 MESH = pl.DeviceIdType.MESH
-PER_STEP = SWEEPS + 3
-MESSAGES = 2 + STEPS * PER_STEP
+MOB = STEPS * SWEEPS + 1
+WARM, CURE = MOB + STEPS, MOB + 2 * STEPS
+FILL = MOB + 3 * STEPS
+MESSAGES = FILL + 1
 
 
 def mobility_of(warmth, cure, preform):
@@ -124,72 +126,62 @@
     def edge_rows(m, p):
         return jnp.where(edge_row, hr[m, p], 0.0)
 
-    P0, FILL = 0, 1
-    MOB = [2 + s * PER_STEP for s in range(STEPS)]
-    WARM = [m + 1 for m in MOB]
-    CURE = [m + 2 for m in MOB]
-    PRESS = [[MOB[s] + 3 + k for k in range(SWEEPS)] for s in range(STEPS)]
-    sources = {P0: pb.at[0], FILL: fill}
-    for s in range(STEPS):
-        sources[MOB[s]], sources[WARM[s]], sources[CURE[s]] = mb.at[s], tb.at[s], cb.at[s]
-        for k in range(SWEEPS):
-            sources[PRESS[s][k]] = pb.at[s * SWEEPS + k + 1]
-
-    def reduce_send(s):
+    def reduce_send():
         def body(off, carry):
             pltpu.make_async_remote_copy(
-                src_ref=part.at[s], dst_ref=red.at[s, tile],
-                send_sem=rs_sem.at[s, off], recv_sem=rr_sem.at[s, tile],
+                src_ref=part, dst_ref=red.at[tile],
+                send_sem=rs_sem.at[off], recv_sem=rr_sem.at[tile],
                 device_id=(ply, lax.rem(tile + off, n_tile)), device_id_type=MESH,
             ).start()
             return carry
 
         lax.fori_loop(1, n_tile, body, 0)
 
-    def reduce_mid(s):
+    def reduce_mid():
         def body(off, total):
             peer = lax.rem(tile + off, n_tile)
             copy = pltpu.make_async_remote_copy(
-                src_ref=part.at[s], dst_ref=red.at[s, peer],
-                send_sem=rs_sem.at[s, off], recv_sem=rr_sem.at[s, peer],
+                src_ref=part, dst_ref=red.at[peer],
+                send_sem=rs_sem.at[off], recv_sem=rr_sem.at[peer],
                 device_id=(ply, peer), device_id_type=MESH,
             )
             copy.wait_recv()
             copy.wait_send()
-            return total + red[s, peer]
-
-        half[s] = lax.fori_loop(1, n_tile, body, part[s])
+            return total + red[peer]
+
+        half[...] = lax.fori_loop(1, n_tile, body, part[...])
         for off in range(1, n_ply):
             pltpu.make_async_remote_copy(
-                src_ref=half.at[s], dst_ref=tot.at[s, ply],
-                send_sem=qs_sem.at[s, off], recv_sem=qr_sem.at[s, ply],
+                src_ref=half, dst_ref=tot.at[ply],
+                send_sem=qs_sem.at[off], recv_sem=qr_sem.at[ply],
                 device_id=(lax.rem(ply + off, n_ply), tile), device_id_type=MESH,
             ).start()
 
-    def reduce_end(s):
-        tot[s, ply] = half[s]
+    def reduce_end():
+        tot[ply] = half[...]
         for off in range(1, n_ply):
             peer = lax.rem(ply + off, n_ply)
             copy = pltpu.make_async_remote_copy(
-                src_ref=half.at[s], dst_ref=tot.at[s, peer],
-                send_sem=qs_sem.at[s, off], recv_sem=qr_sem.at[s, peer],
+                src_ref=half, dst_ref=tot.at[peer],
+                send_sem=qs_sem.at[off], recv_sem=qr_sem.at[peer],
                 device_id=(peer, tile), device_id_type=MESH,
             )
             copy.wait_recv()
             copy.wait_send()
-        total = tot[s, 0]
+        total = tot[0]
         for j in range(1, n_ply):
-            total = total + tot[s, j]
-        root = jnp.sqrt(jnp.full((8, 128), jnp.sum(total)) / sites + epsilon)
-        rec_out[s] = root[0, 0]
+            total = total + tot[j]
+        for s in range(STEPS):
+            root = jnp.sqrt(jnp.full((8, 128), jnp.sum(total[s])) / sites + epsilon)
+            rec_out[s] = root[0, 0]
 
     ins[0].wait()
-    send(P0, pb.at[0])
+    send(0, pb.at[0])
     for copy in ins[1:4]:
         copy.wait()
     for p in range(planes):
         mb[0, p] = mobility_of(tb[0, p], cb[0, p], kb[p])
-    send(MOB[0], mb.at[0])
+    send(MOB, mb.at[0])
     for copy in ins[4:]:
         copy.wait()
     for p in range(planes):
@@ -204,8 +196,7 @@
         fills[2, p] = jnp.where(last_lane, 0.0, up(wet, 1))
         fills[3, p] = jnp.where(first_lane, 0.0, down(wet, 1))
 
-    before = P0
-    for s in range(STEPS):
+    def time_step(s, carry):
         for p in range(planes):
             m = mb[s, p]
             if p:
@@ -216,6 +207,16 @@
             b = jnp.where(last_lane, 0.0, face(m, up(m, 1)))
             fx[0, p] = b
             fx[1, p] = jnp.where(first_lane, 0.0, down(b, 1))
+        landed(MOB + s, mb.at[s], (2, 3, 0, 1))
+        fz[0] = face(mb[s, 0], low_plane(MOB + s))
+        fz[planes] = face(mb[s, planes - 1], high_plane(MOB + s))
+        for p in range(planes):
+            beside = face(mb[s, p], edge_rows(MOB + s, p))
+            fh[p] = beside
+            total = fz[p] + fz[p + 1] + fy[0, p] + fy[1, p] + beside + fx[0, p] + fx[1, p]
+            diag[p] = total
+            moving = free[p] > 0
+            inv[p] = jnp.where(moving, 1.0 / jnp.where(moving, total, 1.0), 0.0)
 
         def inside(x):
             for p in range(planes):
@@ -228,65 +229,53 @@
                     total += fz[p + 1] * x[p + 1]
                 acc[p] = total
 
-        inside(pb.at[s * SWEEPS])
-        landed(MOB[s], mb.at[s], (2, 3, 0, 1))
-        fz[0] = face(mb[s, 0], low_plane(MOB[s]))
-        fz[planes] = face(mb[s, planes - 1], high_plane(MOB[s]))
-        for p in range(planes):
-            beside = face(mb[s, p], edge_rows(MOB[s], p))
-            fh[p] = beside
-            total = fz[p] + fz[p + 1] + fy[0, p] + fy[1, p] + beside + fx[0, p] + fx[1, p]
-            diag[p] = total
-            moving = free[p] > 0
-            inv[p] = jnp.where(moving, 1.0 / jnp.where(moving, total, 1.0), 0.0)
-
-        order = list(range(1, planes - 1))
-        for k in range(SWEEPS):
-            old, new = pb.at[s * SWEEPS + k], pb.at[s * SWEEPS + k + 1]
-            if s == 0 or k:
-                landed(before, old, (2, 3))
+        def arrive(j, ds, fresh):
+            for d in ds:
+                pl.when(has[d] & fresh)(lambda d=d: message(j, pb.at[j], d).wait_recv())
+
+        def sweep(k, carry):
+            j = s * SWEEPS + k
+            old, new = pb.at[j], pb.at[j + 1]
+            fresh = (s == 0) | (k > 0)
+            inside(old)
+            arrive(j, (2, 3), fresh)
 
             def finish(p):
-                total = acc[p] + fh[p] * edge_rows(before, p)
+                total = acc[p] + fh[p] * edge_rows(j, p)
                 if p == 0:
-                    total += fz[0] * low_plane(before)
+                    total += fz[0] * low_plane(j)
                 if p == planes - 1:
-                    total += fz[planes] * high_plane(before)
+                    total += fz[planes] * high_plane(j)
                 new[p] = total * inv[p] + fixed[p]
 
-            for p in order:
+            for p in range(1, planes - 1):
                 finish(p)
             if planes > 1:
-                if s == 0 or k:
-                    landed(before, old, (1,))
+                arrive(j, (1,), fresh)
                 finish(0)
-                send(PRESS[s][k], new, (0,))
-                if s == 0 or k:
-                    landed(before, old, (0,))
+                send(j + 1, new, (0,))
+                arrive(j, (0,), fresh)
                 finish(planes - 1)
-                send(PRESS[s][k], new, (1, 2, 3))
+                send(j + 1, new, (1, 2, 3))
             else:
-                if s == 0 or k:
-                    landed(before, old, (0, 1))
+                arrive(j, (0, 1), fresh)
                 finish(0)
-                send(PRESS[s][k], new)
-            if k == 0:
-                send(WARM[s], tb.at[s])
-            if k == 1:
-                send(CURE[s], cb.at[s])
-            if k == 2 and s == 0:
-                send(FILL, fill)
-            if k == 1 and s:
-                reduce_mid(s - 1)
-            inside(new)
-            before = PRESS[s][k]
-
-        now = s * SWEEPS + SWEEPS
-        if s == STEPS - 1:
-            pltpu.make_async_copy(pb.at[now], p_out, out_sem.at[0]).start()
-        landed(WARM[s], tb.at[s], (0, 1, 2, 3))
-        landed(CURE[s], cb.at[s], (0, 1, 2, 3))
-        if s == 0:
+                send(j + 1, new)
+            pl.when(k == 0)(lambda: send(WARM + s, tb.at[s]))
+            pl.when(k == 1)(lambda: send(CURE + s, cb.at[s]))
+            pl.when((k == 2) & (s == 0))(lambda: send(FILL, fill))
+            return carry
+
+        lax.fori_loop(0, SWEEPS, sweep, 0)
+
+        now = (s + 1) * SWEEPS
+        last = s == STEPS - 1
+        inside(pb.at[now])
+        landed(WARM + s, tb.at[s], (0, 1, 2, 3))
+        landed(CURE + s, cb.at[s], (0, 1, 2, 3))
+
+        @pl.when(s == 0)
+        def _():
             landed(FILL, fill, (0, 1, 2, 3))
 
         def stream(p, f, press, warm, cure, wet):
@@ -294,7 +283,6 @@
             dt = warm - tb[s, p]
             return (q + diffusion_coefficient * wet) * dt, q * (cure - cb[s, p])
 
-        gained = []
         for p in range(planes):
             v, t, c = pb[now, p], tb[s, p], cb[s, p]
             speed = arrhenius_prefactor * jnp.exp(arrhenius_barrier * (1.0 - 1.0 / t)) * (1.0 - c)
@@ -311,14 +299,14 @@
             tb[s + 1, p] = dt
             cb[s + 1, p] = dc
 
-        landed(before, pb.at[now], (2, 3, 0, 1))
+        landed(now, pb.at[now], (2, 3, 0, 1))
         squares = jnp.zeros((rows, width), jnp.float32)
         for p in range(planes):
-            total = acc[p] + fh[p] * edge_rows(before, p)
+            total = acc[p] + fh[p] * edge_rows(now, p)
             if p == 0:
-                total += fz[0] * low_plane(before)
+                total += fz[0] * low_plane(now)
             if p == planes - 1:
-                total += fz[planes] * high_plane(before)
+                total += fz[planes] * high_plane(now)
             off = free[p] * (total - diag[p] * pb[now, p])
             squares += off * off
         small = jnp.zeros((8, 128), jnp.float32)
@@ -326,18 +314,17 @@
             for l in range(0, width, 128):
                 small += squares[r:r + 8, l:l + 128]
         part[s] = small
-        if s == STEPS - 1:
-            reduce_send(s)
+        pl.when(last)(reduce_send)
         for p in range(planes):
             dt, dc = tb[s + 1, p], cb[s + 1, p]
-            ways = [(fh[p], edge_rows(before, p), edge_rows(WARM[s], p), edge_rows(CURE[s], p),
+            ways = [(fh[p], edge_rows(now, p), edge_rows(WARM + s, p), edge_rows(CURE + s, p),
                      edge_rows(FILL, p))]
             if p == 0:
-                ways.append((fz[0], low_plane(before), low_plane(WARM[s]), low_plane(CURE[s]),
+                ways.append((fz[0], low_plane(now), low_plane(WARM + s), low_plane(CURE + s),
                              low_plane(FILL)))
             if p == planes - 1:
-                ways.append((fz[planes], high_plane(before), high_plane(WARM[s]),
-                             high_plane(CURE[s]), high_plane(FILL)))
+                ways.append((fz[planes], high_plane(now), high_plane(WARM + s),
+                             high_plane(CURE + s), high_plane(FILL)))
             for way in ways:
                 a, b = stream(p, *way)
                 dt, dc = dt + a, dc + b
@@ -346,25 +333,27 @@
             c = cb[s, p] + share * dc
             tb[s + 1, p] = t
             cb[s + 1, p] = c
-            if s < STEPS - 1:
-                mb[s + 1, p] = mobility_of(t, c, kb[p])
-        if s < STEPS - 1:
-            send(MOB[s + 1], mb.at[s + 1])
-            reduce_send(s)
+            mb[s + 1, p] = mobility_of(t, c, kb[p])
+        pl.when(s < STEPS - 1)(lambda: send(MOB + s + 1, mb.at[s + 1]))
+        return carry
+
+    lax.fori_loop(0, STEPS, time_step, 0)
 
     outs = [
         pltpu.make_async_copy(pb.at[STEPS * SWEEPS], p_out, out_sem.at[0]),
         pltpu.make_async_copy(tb.at[STEPS], t_out, out_sem.at[1]),
         pltpu.make_async_copy(cb.at[STEPS], c_out, out_sem.at[2]),
     ]
-    outs[1].start()
-    outs[2].start()
-    reduce_mid(STEPS - 1)
-    for s in range(STEPS - 1):
-        reduce_end(s)
-    for m, src in sources.items():
-        sent(m, src)
-    reduce_end(STEPS - 1)
+    for copy in outs:
+        copy.start()
+    reduce_mid()
+
+    def drain(m, carry):
+        sent(m, pb.at[0])
+        return carry
+
+    lax.fori_loop(0, MESSAGES, drain, 0)
+    reduce_end()
     for copy in outs:
         copy.wait()
 
@@ -379,15 +368,15 @@
 
     dma = pltpu.SemaphoreType.DMA
     scratch = [
-        block(STEPS + 1), block(STEPS + 1), block(STEPS * SWEEPS + 1), block(STEPS), block(),
+        block(STEPS + 1), block(STEPS + 1), block(STEPS * SWEEPS + 1), block(STEPS + 1), block(),
         pltpu.VMEM((3, *shape), jnp.int32), block(), block(), block(), block(4),
         pltpu.VMEM((planes + 1, rows, width), real), block(2), block(2), block(), block(), block(),
         block(), pltpu.VMEM((STEPS, 8, 128), real),
         pltpu.VMEM((MESSAGES, 2, rows, width), real), block(MESSAGES),
-        pltpu.VMEM((STEPS, n_tile, 8, 128), real), pltpu.VMEM((STEPS, 8, 128), real),
-        pltpu.VMEM((STEPS, n_ply, 8, 128), real),
+        pltpu.VMEM((n_tile, STEPS, 8, 128), real), pltpu.VMEM((STEPS, 8, 128), real),
+        pltpu.VMEM((n_ply, STEPS, 8, 128), real),
         dma((7,)), dma((3,)), dma((MESSAGES, 4)), dma((MESSAGES, 4)),
-        dma((STEPS, n_tile)), dma((STEPS, n_tile)), dma((STEPS, n_ply)), dma((STEPS, n_ply)),
+        dma((n_tile,)), dma((n_tile,)), dma((n_ply,)), dma((n_ply,)),
     ]
     out = jax.ShapeDtypeStruct(shape, real)
     anywhere = pl.BlockSpec(memory_space=pl.ANY)
@@ -398,7 +387,7 @@
         out_specs=(anywhere, anywhere, anywhere, pl.BlockSpec(memory_space=pltpu.SMEM)),
         scratch_shapes=scratch,
         compiler_params=pltpu.CompilerParams(
-            collective_id=0, has_side_effects=True, vmem_limit_bytes=24 * 1024 * 1024
+            collective_id=0, has_side_effects=True, vmem_limit_bytes=60 * 1024 * 1024
         ),
     )(*fields)
 

time: 61.1 us -> 54.9 us (0.90)
  local copies, waits for them, and re-layouts: 8.8 us -> 3.73 us
  Pallas kernels: 51.4 us -> 50.4 us
    unnamed x18 -> x10, local copies, waits for them, and re-layouts: 8.8 us -> 3.73 us
    pallas_call x1, Pallas kernels: 51.4 us -> 50.4 us  [per_device(): pl.pallas_call(functools.partial(kernel, n_ply, n_tile), out_shape=(out,...]
where the time goes in v2:
time: 54.9 us; the launch traced here: 54.8 us
  Pallas kernels  50.4 us (92%)
  local copies, waits for them, and re-layouts  3.73 us (7%)
  between operations  0.65 us (1%)
    pallas_call x1, Pallas kernels, per_device(): pl.pallas_call(functools.partial(kernel, n_ply, n_tile), out_shape=(out,...  50.4 us
    unnamed x10, local copies, waits for them, and re-layouts  3.73 us

profile of v2, /device:TPU:0, one launch (start us, length us, event | category | flops | bytes accessed | tf_op | source)
XLA Modules:
  0.0 54.8 jit_solution(17391265717647239695)
XLA Ops:
  0.6 50.4 %shard_map.102 = (f32[4,8,1024]{2,1,0:T(8,128)}, f32[4,8,1024]{2,1,0:T(8,128)}, f32[4,8,1024]{2,1,0:T(8,128)}, f32[2]{0:T(128)}) custom-call(f32[4,8,1024]{2,1,0:T(8,128)} %t_in.1, f32[4,8,1024]{2,1,0:T(8,128)} %c_in.1, f32[4,8,1024]{2,1,0:T(8,128)} %p_in.1, f32[4,8,1024]{2,1,0:T(8,128)} %k_in.1, s32[4,8,1024]{2,1,0:T(8,128)} %w_in.1, s32[4,8,1024]{2,1,0:T(8,128)} %i_in.1, ...), custom_call_target="tpu_custom_call" | custom-call | tf_op jit(solution)/shard_map/pallas_call | solution.py:383
  51.0 0.0 copy-start.1
  51.0 1.6 %copy.15 = f32[4,8,1024]{2,1,0:T(8,128)} copy(f32[4,8,1024]{2,1,0:T(8,128)} %get-tuple-element.8) | data formatting | bytes 262144
  52.6 0.0 copy-done.1
  52.6 0.0 copy-start
  52.6 0.7 %copy.16 = f32[4,8,1024]{2,1,0:T(8,128)} copy(f32[4,8,1024]{2,1,0:T(8,128)S(1)} %copy-done.1) | data formatting | bytes 262144
  53.3 0.3 copy-done
  53.6 0.0 copy-start.2
  53.6 0.7 %copy.17 = f32[4,8,1024]{2,1,0:T(8,128)} copy(f32[4,8,1024]{2,1,0:T(8,128)S(1)} %copy-done) | data formatting | bytes 262144
  54.3 0.0 copy-done.2
  54.3 0.5 copy.18
Async XLA Ops:
  51.0 1.6 %copy-start.1 = (f32[4,8,1024]{2,1,0:T(8,128)S(1)}, f32[4,8,1024]{2,1,0:T(8,128)}, u32[]{:S(2)}) copy-start(f32[4,8,1024]{2,1,0:T(8,128)} %get-tuple-element.9) | copy-start | bytes 393220
  52.6 1.0 %copy-start = (f32[4,8,1024]{2,1,0:T(8,128)S(1)}, f32[4,8,1024]{2,1,0:T(8,128)}, u32[]{:S(2)}) copy-start(f32[4,8,1024]{2,1,0:T(8,128)} %get-tuple-element.10) | copy-start | bytes 393220
  53.6 0.7 %copy-start.2 = (f32[2]{0:T(128)S(1)}, f32[2]{0:T(128)}, u32[]{:S(2)}) copy-start(f32[2]{0:T(128)} %get-tuple-element.11) | copy-start | bytes 28

commit v3 on v2

--- a/solution.py
+++ b/solution.py
@@ -358,6 +358,14 @@
         copy.wait()
 
 
+def hand_over(t_in, c_in, p_in, rec_in, t_out, c_out, p_out, rec_out):
+    t_out[...] = t_in[...]
+    c_out[...] = c_in[...]
+    p_out[...] = p_in[...]
+    for s in range(STEPS):
+        rec_out[s] = rec_in[s]
+
+
 def per_device(n_ply, n_tile, *fields):
     shape = fields[0].shape
     planes, rows, width = shape
@@ -380,7 +388,7 @@
     ]
     out = jax.ShapeDtypeStruct(shape, real)
     anywhere = pl.BlockSpec(memory_space=pl.ANY)
-    return pl.pallas_call(
+    results = pl.pallas_call(
         functools.partial(kernel, n_ply, n_tile),
         out_shape=(out, out, out, jax.ShapeDtypeStruct((STEPS,), real)),
         in_specs=[anywhere] * 7,
@@ -390,6 +398,14 @@
             collective_id=0, has_side_effects=True, vmem_limit_bytes=60 * 1024 * 1024
         ),
     )(*fields)
+    scalars = pl.BlockSpec(memory_space=pltpu.SMEM)
+    return pl.pallas_call(
+        hand_over,
+        out_shape=(out, out, out, jax.ShapeDtypeStruct((STEPS,), real)),
+        in_specs=[pl.BlockSpec(memory_space=pltpu.VMEM)] * 3 + [scalars],
+        out_specs=(*[pl.BlockSpec(memory_space=pltpu.VMEM)] * 3, scalars),
+        compiler_params=pltpu.CompilerParams(vmem_limit_bytes=60 * 1024 * 1024),
+    )(*results)
 
 
 def solution(mesh):

time: 54.9 us -> 53 us (0.965)
  local copies, waits for them, and re-layouts: 3.73 us -> 0 us
  Pallas kernels: 50.4 us -> 52.2 us
    unnamed x10 -> x0, local copies, waits for them, and re-layouts: 3.73 us -> none
    pallas_call x0 -> x1, Pallas kernels: none -> 1.8 us  [per_device(): pl.pallas_call(hand_over, out_shape=(out, out, out, jax.ShapeDtypeStruct(...]
where the time goes in v3:
time: 53 us; the launch traced here: 52.8 us
  Pallas kernels  52.2 us (98%)
  between operations  0.64 us (1%)
    pallas_call x1, Pallas kernels, per_device(): pl.pallas_call(functools.partial(kernel, n_ply, n_tile), out_shape=(out,...  50.4 us
    pallas_call x1, Pallas kernels, per_device(): pl.pallas_call(hand_over, out_shape=(out, out, out, jax.ShapeDtypeStruct(...  1.8 us

profile of v3, /device:TPU:0, one launch (start us, length us, event | category | flops | bytes accessed | tf_op | source)
XLA Modules:
  0.0 52.8 jit_solution(4131490045780934220)
XLA Ops:
  0.6 50.4 %shard_map.102 = (f32[4,8,1024]{2,1,0:T(8,128)}, f32[4,8,1024]{2,1,0:T(8,128)}, f32[4,8,1024]{2,1,0:T(8,128)}, f32[2]{0:T(128)}) custom-call(f32[4,8,1024]{2,1,0:T(8,128)} %t_in.1, f32[4,8,1024]{2,1,0:T(8,128)} %c_in.1, f32[4,8,1024]{2,1,0:T(8,128)} %p_in.1, f32[4,8,1024]{2,1,0:T(8,128)} %k_in.1, s32[4,8,1024]{2,1,0:T(8,128)} %w_in.1, s32[4,8,1024]{2,1,0:T(8,128)} %i_in.1, ...), custom_call_target="tpu_custom_call" | custom-call | tf_op jit(solution)/shard_map/pallas_call | solution.py:391
  51.0 1.8 %shard_map.103 = (f32[4,8,1024]{2,1,0:T(8,128)}, f32[4,8,1024]{2,1,0:T(8,128)}, f32[4,8,1024]{2,1,0:T(8,128)}, f32[2]{0:T(128)}) custom-call(f32[4,8,1024]{2,1,0:T(8,128)} %get-tuple-element.8.t_in, f32[4,8,1024]{2,1,0:T(8,128)} %get-tuple-element.9.c_in, f32[4,8,1024]{2,1,0:T(8,128)} %get-tuple-element.10.p_in, f32[2]{0:T(128)} %get-tuple-element.11.rec_in), custom_call_target="tpu_custom_call" | custom-call | tf_op jit(solution)/shard_map/pallas_call | solution.py:402
